TPU v7x, 32 devices: a whole 2x2x4 slice. The times are simulated.
32 devices in a mesh: ctx: 4 (over y, x), head: 4 (over z), var: 2 (over core).
Axes of the slice: x: 2, y: 2, z: 4, core: 2. Of those that a mesh axis runs over, the one named last changes fastest.
Arguments:
- sequence: bfloat16 [2048, 1536], P('ctx', 'head'), may hold values from -8 to 8
- deletions: int32 [8, 2], P('var'), parts along dimension 0, may hold values from 0 to 2048, as said below
- conv_taps: float32 [3, 1536], P(None, 'head'), may hold values from -3 to 3
- conv_bias: float32 [1536], P('head'), may hold values from -3 to 3
- w_proj: bfloat16 [1536, 3584], P(None, 'head'), may hold values from -1 to 1
- w_out: bfloat16 [1536, 1536], P('head'), may hold values from -0.15625 to 0.15625
- w_pair: bfloat16 [1536, 256], P('head'), may hold values from -0.15625 to 0.15625
- dist_table: float32 [16, 128], replicated, may hold values from -3 to 3
Outputs:
- pair_map: bfloat16 [8, 512, 512, 128], P('var', 'ctx', 'head'), parts along dimension 0
There are 2 independent parts, one for each index of `var`. A program takes and returns all parts, laid end to end along the dimension named above; an argument that names none is the same for every part. Nothing has to cross between parts.
Inputs may be any that keep to these rules, and one draw needn't show every extreme that they name: `deletions`: each variant deletes 1 to 128 consecutive tokens, some variant deletes exactly 128, and some variant's deletion ends at the last token of the locus.
All inputs are finite; a program needn't handle non-finite values.
Results may differ from a plain program's by a relative error of at most 0.025.
Values may be sent and summed in bfloat16 or wider, within the bound.
No kernel may reach another device: no remote copies, remote signals or barrier semaphores. Data moves between devices by JAX's collectives and lax.ppermute only.
A program may use at most 128 MiB of HBM per device.

v0:
```python
import math

import jax
import jax.numpy as jnp
from jax import lax
from jax.sharding import PartitionSpec as P

HD = 128
VD = 192
C = 128
NB = 16
POOL = 4


def extended(block, sides, width):
    for axis, dim in sides:
        count = lax.axis_size(axis)
        forward = [(i, i + 1) for i in range(count - 1)]
        backward = [(target, source) for source, target in forward]
        low = lax.ppermute(
            lax.slice_in_dim(block, block.shape[dim] - width, None, axis=dim), axis, forward
        )
        high = lax.ppermute(lax.slice_in_dim(block, 0, width, axis=dim), axis, backward)
        block = jnp.concatenate([low, block, high], axis=dim)
    return block


def attend_block(running, queries, key_rows, value_rows):
    row_max, row_sum, weighted = running
    scores = jnp.einsum(
        "vqhe,vkhe->vhqk", queries, key_rows, preferred_element_type=jnp.float32
    ) / math.sqrt(queries.shape[-1])
    new_max = jnp.maximum(row_max, scores.max(-1))
    shrink = jnp.exp(row_max - new_max)
    weights = jnp.exp(scores - new_max[..., None])
    row_sum = row_sum * shrink + weights.sum(-1)
    weighted = weighted * shrink[..., None] + jnp.einsum(
        "vhqk,vkhe->vhqe",
        weights.astype(jnp.bfloat16),
        value_rows,
        preferred_element_type=jnp.float32,
    )
    return (new_max, row_sum, weighted)


def attend_rows(running, queries, key_rows, value_rows):
    key_total = key_rows.shape[1]
    block_rows = 512
    block_count = key_total // block_rows

    def block_step(block_index, state_now):
        key_part = lax.dynamic_slice_in_dim(key_rows, block_index * block_rows, block_rows, 1)
        value_part = lax.dynamic_slice_in_dim(value_rows, block_index * block_rows, block_rows, 1)
        return attend_block(state_now, queries, key_part, value_part)

    return lax.fori_loop(0, block_count, block_step, running)


def local(sequence, deletions, conv_taps, conv_bias, w_proj, w_out, w_pair, dist_table):
    token_count, local_width = sequence.shape
    variants = deletions.shape[0]
    head_count = w_out.shape[0] // VD
    row_start = lax.axis_index("ctx") * token_count
    positions = row_start + jnp.arange(token_count, dtype=jnp.int32)
    kept = jnp.logical_or(
        positions[None, :] < deletions[:, 0:1], positions[None, :] >= deletions[:, 1:2]
    )
    masked = jnp.where(kept[:, :, None], sequence[None], jnp.zeros((), jnp.bfloat16))
    dilation = token_count // 2
    padded = extended(masked, (("ctx", 1),), dilation)
    spread = padded.astype(jnp.float32)
    middle = spread[:, dilation : dilation + token_count]
    convolved = (
        conv_taps[0] * spread[:, :token_count]
        + conv_taps[1] * middle
        + conv_taps[2] * spread[:, 2 * dilation : 2 * dilation + token_count]
        + conv_bias
    )
    trunk_out = (middle + jax.nn.gelu(convolved, approximate=True)).astype(jnp.bfloat16)
    projected = jnp.einsum(
        "vtd,df->vtf",
        lax.all_gather(trunk_out, "head", axis=2, tiled=True),
        w_proj,
        preferred_element_type=jnp.float32,
    ).astype(jnp.bfloat16)
    projected = projected.reshape(trunk_out.shape[0], token_count, head_count, 2 * HD + VD)
    queries = projected[:variants, :, :, :HD]
    key_rows = projected[:, :, :, HD : 2 * HD]
    value_rows = projected[:, :, :, 2 * HD :]
    running = attend_rows(
        (
            jnp.full((variants, head_count, token_count), -jnp.inf, jnp.float32),
            jnp.zeros((variants, head_count, token_count), jnp.float32),
            jnp.zeros((variants, head_count, token_count, VD), jnp.float32),
        ),
        queries,
        lax.all_gather(key_rows, "ctx", axis=1, tiled=True),
        lax.all_gather(value_rows, "ctx", axis=1, tiled=True),
    )
    row_max, row_sum, weighted = running
    head_out = (weighted / row_sum[..., None]).astype(jnp.bfloat16)
    flat_out = head_out.transpose(0, 2, 1, 3).reshape(variants * token_count, head_count * VD)
    mixed_back = lax.psum_scatter(
        lax.dot_general(
            w_out, flat_out, (((0,), (1,)), ((), ())), preferred_element_type=jnp.float32
        ).astype(jnp.bfloat16),
        "head",
        scatter_dimension=0,
        tiled=True,
    ).astype(jnp.float32)
    residual = trunk_out.astype(jnp.float32) + mixed_back.T.reshape(
        variants, token_count, local_width
    )
    pooled = (
        residual.reshape(variants, token_count // POOL, POOL, local_width)
        .mean(2)
        .astype(jnp.bfloat16)
    )
    partial_value = jnp.einsum("vpd,dc->vpc", pooled, w_pair, preferred_element_type=jnp.float32)
    pair_proj = lax.psum(partial_value.astype(jnp.bfloat16), "head").astype(jnp.float32)
    row_feats = pair_proj[:, :, :C]
    all_cols = lax.all_gather(
        pair_proj[:, :, C:].astype(jnp.bfloat16), "ctx", axis=1, tiled=True
    ).astype(jnp.float32)
    col_count = all_cols.shape[1] // lax.axis_size("head")
    col_start = lax.axis_index("head") * col_count
    col_feats = lax.dynamic_slice_in_dim(all_cols, col_start, col_count, 1)
    row_ids = lax.axis_index("ctx") * (token_count // POOL) + jnp.arange(
        token_count // POOL, dtype=jnp.int32
    )
    col_ids = col_start + jnp.arange(col_count, dtype=jnp.int32)
    distance = jnp.abs(row_ids[:, None] - col_ids[None, :])
    buckets = jnp.zeros(distance.shape, jnp.int32)
    for power_index in range(NB - 1):
        buckets = buckets + (distance >= 2**power_index).astype(jnp.int32)
    one_hot = (buckets[:, :, None] == jnp.arange(NB, dtype=jnp.int32)).astype(jnp.float32)
    rel_table = jnp.dot(one_hot, dist_table, precision=lax.Precision.HIGHEST)
    pair_map = row_feats[:, :, None, :] + col_feats[:, None, :, :] + rel_table[None]
    return pair_map.astype(jnp.bfloat16)


def solution(mesh):
    in_specs = (
        P("ctx", "head"),
        P("var", None),
        P(None, "head"),
        P("head"),
        P(None, "head"),
        P("head", None),
        P("head", None),
        P(),
    )
    out_specs = P("var", "ctx", "head", None)
    return jax.shard_map(local, mesh=mesh, in_specs=in_specs, out_specs=out_specs, check_vma=False)
```

profile of v0, /device:TPU:0, one launch (start us, length us, event | category | flops | bytes accessed | tf_op | source)
XLA Modules:
  0.0 595.9 jit_solution(169889997960448816)
XLA Ops:
  6.5 0.9 slice_bitcast_fusion.1
  7.5 1.4 broadcast_select_fusion.1
  9.0 4.9 collective-permute-start
  13.9 1.3 collective-permute-start.1
  15.3 15.4 %collective-permute-done = bf16[4,256,384]{2,1,0:T(8,128)(2,1)S(1)} collective-permute-done((bf16[4,256,384]{2,1,0:T(8,128)(2,1)S(1)}, bf16[4,256,384]{2,1,0:T(8,128)(2,1)S(1)}, u32[]{:S(2)}, u32[]{:S(2)}) %collective-permute-start) | collective-permute-done | bytes 786464 | tf_op jit(solution)/shard_map/ppermute | solution.py:20
  30.7 18.8 %collective-permute-done.1 = bf16[4,256,384]{2,1,0:T(8,128)(2,1)S(1)} collective-permute-done((bf16[4,256,384]{2,1,0:T(8,128)(2,1)S(1)}, bf16[4,256,384]{2,1,0:T(8,128)(2,1)S(1)}, u32[]{:S(2)}, u32[]{:S(2)}) %collective-permute-start.1) | collective-permute-done | bytes 786464 | tf_op jit(solution)/shard_map/ppermute | solution.py:23
  49.9 2.6 copy-done.3
  52.5 2.6 fusion.27
  55.3 115.8 %all-gather.4.cloned.1.call-done = bf16[4,512,1536]{2,1,0:T(8,128)(2,1)} async-done(((bf16[4,512,384]{2,1,0:T(8,128)(2,1)}), bf16[4,512,1536]{2,1,0:T(8,128)(2,1)}) %all-gather.4.cloned.1.call-update) | async-done | bytes 6291472 | tf_op jit(solution)/shard_map/all_gather | solution.py:82
  171.0 9.9 %fusion.33 = bf16[4,512,896]{2,1,0:T(8,128)(2,1)} fusion(bf16[4,512,1536]{2,1,0:T(8,128)(2,1)} %all-gather.4.cloned.1.call-done, bf16[1536,896]{1,0:T(8,128)(2,1)S(1)} %copy-done), kind=kOutput, calls=%fused_computation.44 | convolution fusion | flops 5638979584 | bytes 12713984 | tf_op jit(solution)/shard_map/vtd,df->vtf/dot_general | solution.py:80
  181.0 5.9 copy.19
  186.9 2.7 fusion.58
  189.7 2.7 slice.78
  192.7 0.7 copy.21
  193.3 47.3 %all-gather.6.cloned.1.call-done = bf16[4,2048,2,128]{1,3,2,0:T(8,128)(2,1)} async-done(((bf16[4,512,2,128]{1,3,2,0:T(8,128)(2,1)}), bf16[4,2048,2,128]{1,3,2,0:T(8,128)(2,1)}) %all-gather.6.cloned.1.call-update) | async-done | bytes 4194320 | tf_op jit(solution)/shard_map/all_gather | solution.py:97
  240.6 71.9 %all-gather.8.cloned.1.call-done = bf16[4,2048,2,192]{1,3,2,0:T(8,128)(2,1)} async-done(((bf16[4,512,2,192]{1,3,2,0:T(8,128)(2,1)}), bf16[4,2048,2,192]{1,3,2,0:T(8,128)(2,1)}) %all-gather.8.cloned.1.call-update) | async-done | bytes 6291472 | tf_op jit(solution)/shard_map/all_gather | solution.py:98
  312.5 70.4 %while.18 = (s32[]{:T(128)}, f32[4,2,512]{2,1,0:T(2,128)S(1)}, f32[4,2,512]{2,1,0:T(2,128)S(1)}, f32[4,2,512,192]{2,3,1,0:T(8,128)}, bf16[4,2048,2,128]{1,3,2,0:...) while((s32[]{:T(128)}, f32[4,2,512]{2,1,0:T(2,128)S(1)}, ...), condition=%wide.region_3.4_spmd.clone, body=%wide.region_0.3_spmd.clone.sunk | while | flops 1361334272 | bytes 68944072 | solution.py:56
  312.5 5.9 bitcast_reduce_fusion.2
  318.5 4.9 fusion.75
  323.5 0.8 copy-done.2
  324.2 5.1 fusion.77
  329.4 5.9 bitcast_reduce_fusion.2
  335.4 4.9 fusion.75
  340.3 0.8 copy-done.2
  341.1 6.1 %fusion.77 = f32[4,2,512,192]{2,3,1,0:T(8,128)} fusion(f32[4,2,512,192]{2,3,1,0:T(8,128)} %get-tuple-element.266, f32[4,2,512,512]{3,2,1,0:T(8,128)S(1)} %copy-done.2, f32[4,2,512]{2,1,0:T(2,128)S(1)} %fusion.74, bf16[4,2048,2,192]{1,3,2,0:T(8,128)(2,1)} %get-tuple-element.280, s32[]{:T(128)S(6)} %select_n.20, ...), kind=kOutput, calls=%fused_computation.9.clone.1 | convolution fusion | flops 813957120 | bytes 16285701 | tf_op jit(solution)/shard_map/while/body/eval_jaxpr/vhqk,vkhe->vhqe/dot_general | solution.py:37
  347.2 5.9 bitcast_reduce_fusion.2
  353.2 4.9 fusion.75
  358.2 0.8 copy-done.2
  359.0 6.1 %fusion.77 = f32[4,2,512,192]{2,3,1,0:T(8,128)} fusion(f32[4,2,512,192]{2,3,1,0:T(8,128)} %get-tuple-element.266, f32[4,2,512,512]{3,2,1,0:T(8,128)S(1)} %copy-done.2, f32[4,2,512]{2,1,0:T(2,128)S(1)} %fusion.74, bf16[4,2048,2,192]{1,3,2,0:T(8,128)(2,1)} %get-tuple-element.280, s32[]{:T(128)S(6)} %select_n.20, ...), kind=kOutput, calls=%fused_computation.9.clone.1 | convolution fusion | flops 813957120 | bytes 16285701 | tf_op jit(solution)/shard_map/while/body/eval_jaxpr/vhqk,vkhe->vhqe/dot_general | solution.py:37
  365.1 5.9 bitcast_reduce_fusion.2
  371.1 4.9 fusion.75
  376.0 0.8 copy-done.2
  376.8 6.1 %fusion.77 = f32[4,2,512,192]{2,3,1,0:T(8,128)} fusion(f32[4,2,512,192]{2,3,1,0:T(8,128)} %get-tuple-element.266, f32[4,2,512,512]{3,2,1,0:T(8,128)S(1)} %copy-done.2, f32[4,2,512]{2,1,0:T(2,128)S(1)} %fusion.74, bf16[4,2048,2,192]{1,3,2,0:T(8,128)(2,1)} %get-tuple-element.280, s32[]{:T(128)S(6)} %select_n.20, ...), kind=kOutput, calls=%fused_computation.9.clone.1 | convolution fusion | flops 813957120 | bytes 16285701 | tf_op jit(solution)/shard_map/while/body/eval_jaxpr/vhqk,vkhe->vhqe/dot_general | solution.py:37
  382.9 2.3 fusion.36
  385.3 1.2 copy.22
  386.9 5.4 fusion.18
  392.3 8.6 %copy.24 = bf16[1536,2048]{1,0:T(8,128)(2,1)} copy(bf16[1536,2048]{0,1:T(8,128)(2,1)} %fusion.18) | data formatting | bytes 12582912
  401.4 110.4 %reduce-scatter.4.cloned.1.call-done = bf16[384,2048]{1,0:T(8,128)(2,1)} async-done(((bf16[1536,2048]{1,0:T(8,128)(2,1)}), bf16[384,2048]{1,0:T(8,128)(2,1)}) %reduce-scatter.4.cloned.1.call-update) | async-done | bytes 1572880
  511.9 1.9 copy.25
  514.0 5.8 convert_add_fusion
  519.8 4.8 reshape.173
  524.6 3.8 reduce_sum.22
  528.4 1.0 convolution_convert_fusion.1
  529.5 8.9 %fusion.37 = f32[128,128,128]{2,1,0:T(8,128)} fusion(s32[128,128]{1,0:T(8,128)S(1)} %convert_add_fusion.1, f32[16,128]{1,0:T(8,128)S(1)} %copy-done.5), kind=kOutput, calls=%fused_computation.49 | convolution fusion | flops 402915328 | bytes 8462336 | tf_op jit(solution)/shard_map/dot_general | solution.py:137
  538.3 27.1 %all-reduce.2.cloned.1.call-done = bf16[4,128,256]{2,1,0:T(8,128)(2,1)} async-done(((bf16[4,128,256]{2,1,0:T(8,128)(2,1)}), bf16[4,128,256]{2,1,0:T(8,128)(2,1)}) %all-reduce.2.cloned.1.call-update) | async-done | bytes 262160 | tf_op jit(solution)/shard_map/psum | solution.py:120
  565.5 1.0 slice_convert_fusion
  566.5 10.4 %all_gather.15 = bf16[4,512,128]{2,1,0:T(8,128)(2,1)S(1)} all-gather(bf16[4,128,128]{2,1,0:T(8,128)(2,1)S(1)} %get-tuple-element.196), channel_id=1, replica_groups=mesh['ctx'=4,'head'=4,'var'=2] {'ctx'}, dimensions={1}, use_global_device_ids=true | all-gather | bytes 655360 | tf_op jit(solution)/shard_map/all_gather | solution.py:122
  576.9 12.5 %add_convert_fusion = bf16[4,128,128,128]{3,2,1,0:T(8,128)(2,1)} fusion(f32[128,128,128]{2,1,0:T(8,128)} %fusion.37, f32[4,128,128]{2,1,0:T(8,128)S(1)} %dynamic-slice_convert_fusion, f32[4,128,128]{2,1,0:T(8,128)S(1)} %get-tuple-element.195), kind=kLoop, calls=%fused_computation.21 | loop fusion | flops 25165824 | bytes 25690112 | tf_op jit(solution)/shard_map/convert_element_type | solution.py:139
  (54 shorter events, 2.4 us)
Async XLA Ops:
  6.5 164.5 %copy-start = (bf16[1536,896]{1,0:T(8,128)(2,1)S(1)}, bf16[1536,896]{1,0:T(8,128)(2,1)}, u32[]{:S(2)}) copy-start(bf16[1536,896]{1,0:T(8,128)(2,1)} %param.14) | copy-start | bytes 8257540
  6.5 8.7 %copy-start.7 = (f32[3,384]{1,0:T(4,128)S(1)}, f32[3,384]{1,0:T(4,128)}, u32[]{:S(2)}) copy-start(f32[3,384]{1,0:T(4,128)} %param.12) | copy-start | bytes 13828
  6.5 164.5 %all-gather.4.cloned.1.call-start = ((), (), s32[]{:S(2)}) async-start(), calls=%async_computation.1 | async-start | bytes 7864320 | tf_op jit(solution)/shard_map/all_gather | solution.py:82
  9.0 21.6 %collective-permute-start = (bf16[4,256,384]{2,1,0:T(8,128)(2,1)S(1)}, bf16[4,256,384]{2,1,0:T(8,128)(2,1)S(1)}, u32[]{:S(2)}, u32[]{:S(2)}) collective-permute-start(bf16[4,256,384]{2,1,0:T(8,128)(2,1)S(1)} %get-tuple-element.193), channel_id=1, source_target_pairs={{0,8},{8,16},{16,24},{1,9},{9,17},{17,25},{2,10},{10,18},{18,26},{... | collective-permute-start | bytes 2359304 | tf_op jit(solution)/shard_map/ppermute | solution.py:20
  13.9 35.5 %collective-permute-start.1 = (bf16[4,256,384]{2,1,0:T(8,128)(2,1)S(1)}, bf16[4,256,384]{2,1,0:T(8,128)(2,1)S(1)}, u32[]{:S(2)}, u32[]{:S(2)}) collective-permute-start(bf16[4,256,384]{2,1,0:T(8,128)(2,1)S(1)} %get-tuple-element.194), channel_id=1, source_target_pairs={{8,0},{16,8},{24,16},{9,1},{17,9},{25,17},{10,2},{18,10},{26,18},{... | collective-permute-start | bytes 2359304 | tf_op jit(solution)/shard_map/ppermute | solution.py:23
  15.3 37.3 %copy-start.6 = (f32[384]{0:T(512)S(1)}, f32[384]{0:T(512)}, u32[]{:S(2)}) copy-start(f32[384]{0:T(512)} %param.13) | copy-start | bytes 4612
  49.9 2.7 copy-start.3
  55.2 185.4 %all-gather.6.cloned.1.call-start = ((), (), s32[]{:S(2)}) async-start(), calls=%async_computation.2 | async-start | bytes 5242880 | tf_op jit(solution)/shard_map/all_gather | solution.py:97
  189.7 122.8 %all-gather.8.cloned.1.call-start = ((), (), s32[]{:S(2)}) async-start(), calls=%async_computation.3 | async-start | bytes 7864320 | tf_op jit(solution)/shard_map/all_gather | solution.py:98
  192.4 319.5 %reduce-scatter.4.cloned.1.call-start = ((), (), s32[]{:S(2)}) async-start(), calls=%async_computation.5 | async-start | bytes 7864320
  318.5 5.8 copy-start.2
  335.3 5.8 copy-start.2
  353.2 5.8 copy-start.2
  371.0 5.8 copy-start.2
  385.3 1.7 copy-start.8
  401.0 164.5 %all-reduce.2.cloned.1.call-start = ((), (), s32[]{:S(2)}) async-start(), calls=%async_computation.4 | async-start | bytes 524288 | tf_op jit(solution)/shard_map/psum | solution.py:120
  524.6 3.8 copy-start.4
  524.6 4.8 copy-start.5
  576.9 12.5 %copy-start.1 = (bf16[1536,896]{1,0:T(8,128)(2,1)S(1)}, bf16[1536,896]{1,0:T(8,128)(2,1)}, u32[]{:S(2)}) copy-start(bf16[1536,896]{1,0:T(8,128)(2,1)} %param.14) | copy-start | bytes 8257540
Sparse Core Ops, SparseCore 0:
  55.3 115.6 all-gather.3
  189.8 50.7 all-gather.5
  242.5 70.0 all-gather.7
  401.1 110.7 reduce-scatter.3
  529.6 35.8 all-reduce.1
where the time goes:
time: 597 us; the launch traced here: 596 us
  waiting for transfers between devices  407 us (68%)
  matrix products  72.4 us (12%)
  other arithmetic  50.2 us (8%)
  local copies, waits for them, and re-layouts  35.9 us (6%)
  between operations  13.4 us (2%)
  blocking collectives  10.4 us (2%)
  starting transfers between devices  6.75 us (1%)
    all_gather x1, waiting for transfers between devices, local(): lax.all_gather(trunk_out, 'head', axis=2, tiled=True)  116 us
    unnamed x6, waiting for transfers between devices  111 us
    all_gather x1, waiting for transfers between devices, local(): lax.all_gather(value_rows, 'ctx', axis=1, tiled=True)  71.9 us
    all_gather x1, waiting for transfers between devices, local(): lax.all_gather(key_rows, 'ctx', axis=1, tiled=True)  47.3 us
    psum x1, waiting for transfers between devices, local(): lax.psum(partial_value.astype(jnp.bfloat16), 'head').astype(jnp.float32)  27.1 us
    dot_general x4, matrix products, attend_block(): jnp.einsum('vqhe,vkhe->vhqk', queries, key_rows, preferred_element_type=j...  23.8 us
    dot_general x4, matrix products, attend_block(): jnp.einsum('vhqk,vkhe->vhqe', weights.astype(jnp.bfloat16), value_rows, p...  23.5 us
    reduce_sum x4, other arithmetic, attend_block(): row_sum = row_sum * shrink + weights.sum(-1)  19.7 us
  transfers between devices with their start and end apart: 7, of which 7 were waited for; matrix products, arithmetic and copies ran while one was open for 2% of the time, Pallas kernels for 0%

commit v1 on v0

v1 whole, which is shorter than its diff:
```python
import functools
import math

import jax
import jax.numpy as jnp
from jax import lax
from jax.experimental import pallas as pl
from jax.experimental.pallas import tpu as pltpu
from jax.sharding import PartitionSpec as P

HD = 128
VD = 192
VP = 256
C = 128
NB = 16
POOL = 4
WIN = 144
ALIGN = 16
SHIFTS = 8
ROWS = 16
MIB = 1024 * 1024
QSCALE = math.log2(math.e) / math.sqrt(HD)
GELU_A = math.sqrt(2.0 / math.pi)
GELU_B = GELU_A * 0.044715


def trunk_of(taps, low, middle, high):
    convolved = taps[0:1] * low + taps[1:2] * middle + taps[2:3] * high + taps[3:4]
    half = 0.5 * convolved
    bent = jnp.tanh(convolved * (GELU_A + GELU_B * (convolved * convolved)))
    return (middle + (half + half * bent)).astype(jnp.bfloat16)


def masked_trunk(rows, taps, h, start, count, step, first, last):
    tokens = start + lax.broadcasted_iota(jnp.int32, (count, 1), 0)
    parts = []
    for shift in (-step, 0, step):
        part = rows[h, pl.ds(pl.multiple_of(start + step + shift, ALIGN), count), :]
        kept = jnp.logical_or(tokens + shift < first, tokens + shift >= last)
        parts.append(jnp.where(kept, part.astype(jnp.float32), 0.0))
    return trunk_of(taps[h], *parts)


def window_starts(first, step, tokens):
    base = (first // ALIGN) * ALIGN
    return [
        pl.multiple_of(jnp.clip(base + shift, 0, tokens - WIN), ALIGN)
        for shift in (-step, 0, step)
    ]


def pool_matrix(count):
    wide = lax.broadcasted_iota(jnp.int32, (count // POOL, count), 1) // POOL
    tall = lax.broadcasted_iota(jnp.int32, (count // POOL, count), 0)
    return jnp.where(wide == tall, 1.0 / POOL, 0.0).astype(jnp.bfloat16)


def project_kernel(
    heads, dels, place, gathered, taps, weights, base_out, delta_out, pooled_out,
    rows, left, right, sems,
):
    n_ctx, n_head, n_var, step, width = gathered.shape
    tiles = n_ctx * n_var
    tokens = tiles * step
    variants = delta_out.shape[0]
    copies = []
    for tile in range(tiles):
        group = []
        for h in range(n_head):
            copy = pltpu.make_async_copy(
                gathered.at[tile // n_var, h, tile % n_var],
                rows.at[h, pl.ds((tile + 1) * step, step)],
                sems.at[tile, h],
            )
            copy.start()
            group.append(copy)
        copies.append(group)
    rows[:, 0:step] = jnp.zeros((n_head, step, width), jnp.bfloat16)
    rows[:, tokens + step :] = jnp.zeros((n_head, step, width), jnp.bfloat16)
    columns = weights.shape[1]
    at = lax.broadcasted_iota(jnp.int32, (1, columns), 1)
    ones = jnp.zeros((1, columns), jnp.float32)
    scale = jnp.where(at >= heads * (HD + VP), QSCALE, 1.0)
    for h in range(heads):
        ones = jnp.where(at == heads * HD + h * VP + VD, 1.0, ones)

    def wait_tile(tile):
        if tile < tiles:
            for copy in copies[tile]:
                copy.wait()

    def make_tile(tile, into):
        low = tile * step
        for h in range(n_head):
            into[0:step, h * width : (h + 1) * width] = trunk_of(
                taps[h],
                rows[h, low : low + step].astype(jnp.float32),
                rows[h, low + step : low + 2 * step].astype(jnp.float32),
                rows[h, low + 2 * step : low + 3 * step].astype(jnp.float32),
            )

    def make_delta(variant, into):
        first, last = dels[variant, 0], dels[variant, 1]
        for index, start in enumerate(window_starts(first, step, tokens)):
            for h in range(n_head):
                into[index * WIN : (index + 1) * WIN, h * width : (h + 1) * width] = masked_trunk(
                    rows, taps, h, start, WIN, step, first, last
                )

    def project(block, count):
        product = jnp.dot(block[0:count], weights[...], preferred_element_type=jnp.float32)
        return (product * scale + ones).astype(jnp.bfloat16)

    slots = (left, right)
    stages = [("tile", t) for t in range(tiles)] + [("delta", v) for v in range(variants)]

    def make(index):
        kind, which = stages[index]
        if kind == "tile":
            if which == 0:
                wait_tile(0)
            wait_tile(which + 1)
            make_tile(which, slots[index % 2])
        else:
            make_delta(which, slots[index % 2])

    make(0)
    for index, (kind, which) in enumerate(stages):
        if index + 1 < len(stages):
            make(index + 1)
        if kind == "tile":
            base_out[which * step : (which + 1) * step] = project(slots[index % 2], step)
        else:
            delta_out[which] = project(slots[index % 2], 3 * WIN)

    pool = pool_matrix(step)
    mine, ours = place[0], place[1]

    def pool_own(index, carry):
        variant, part = index // n_var, index % n_var
        start = (mine * n_var + part) * step
        block = masked_trunk(
            rows, taps, ours, start, step, step, dels[variant, 0], dels[variant, 1]
        )
        pooled = jnp.dot(pool, block, preferred_element_type=jnp.float32)
        count = step // POOL
        pooled_out[variant, pl.ds(pl.multiple_of(part * count, count), count)] = pooled.astype(
            jnp.bfloat16
        )
        return carry

    lax.fori_loop(0, variants * n_var, pool_own, 0)


def attend_kernel(heads, step, dels, place, base, delta, pooled, w_mix, w_pair, out, kvq):
    tokens = base.shape[0]
    variants = delta.shape[0]
    own = pooled.shape[1] * POOL
    tile = min(own, 256)
    own_start = place[0] * own
    pool = pool_matrix(tile)
    kvq[...] = base[...]

    def scores(h, part):
        low = heads * (HD + VP) + h * HD
        queries = kvq[pl.ds(pl.multiple_of(own_start + part * tile, tile), tile), low : low + HD]
        return lax.dot_general(
            queries,
            kvq[:, h * HD : (h + 1) * HD],
            (((1,), (1,)), ((), ())),
            preferred_element_type=jnp.float32,
        )

    def finish(h, found):
        low = heads * HD + h * VP
        row_max = jnp.max(found, axis=1, keepdims=True)
        weights = jnp.exp2(found - row_max).astype(jnp.bfloat16)
        mixed = jnp.dot(weights, kvq[:, low : low + VP], preferred_element_type=jnp.float32)
        mixed = (mixed * (1.0 / mixed[:, VD : VD + 1])).astype(jnp.bfloat16)
        return jnp.dot(pool, mixed, preferred_element_type=jnp.float32).astype(jnp.bfloat16)

    def one_variant(variant, carry):
        starts = window_starts(dels[variant, 0], step, tokens)
        for index, start in enumerate(starts):
            kvq[pl.ds(start, WIN)] = delta[variant, index * WIN : (index + 1) * WIN]
        chains = [(part, h) for part in range(own // tile) for h in range(heads)]
        ready = scores(chains[0][1], chains[0][0])
        for index, (part, h) in enumerate(chains):
            now = ready
            if index + 1 < len(chains):
                ready = scores(chains[index + 1][1], chains[index + 1][0])
            rows = slice(part * (tile // POOL), (part + 1) * (tile // POOL))
            if h == 0:
                total = jnp.dot(
                    pooled[variant, rows], w_pair[...], preferred_element_type=jnp.float32
                )
            total = total + jnp.dot(
                finish(h, now), w_mix[h], preferred_element_type=jnp.float32
            )
            if h == heads - 1:
                out[variant, rows] = total.astype(out.dtype)
        for start in starts:
            kvq[pl.ds(start, WIN)] = base[pl.ds(start, WIN)]
        return carry

    lax.fori_loop(0, variants, one_variant, 0)


def pair_kernel(place, row_feats, col_feats, table, out):
    block = pl.program_id(0)
    side = col_feats.shape[1]
    rows = table.shape[1] - side
    for r in range(ROWS):
        back = rows - 1 - (block * ROWS + r)
        low = pl.multiple_of((back // SHIFTS) * SHIFTS, SHIFTS)
        relative = table[(rows - 1 - r) % SHIFTS, pl.ds(low, side), :]
        for variant in range(out.shape[0]):
            out[variant, r] = (
                row_feats[variant, r : r + 1, :] + (col_feats[variant] + relative)
            ).astype(jnp.bfloat16)


def distance_table(dist_table, row_start, col_start, rows, cols):
    at = jnp.arange(SHIFTS, dtype=jnp.int32)[:, None] + jnp.arange(
        rows + cols, dtype=jnp.int32
    )
    distance = jnp.abs(row_start - col_start + rows - 1 - at)
    buckets = jnp.zeros(distance.shape, jnp.int32)
    for power_index in range(NB - 1):
        buckets = buckets + (distance >= 2**power_index).astype(jnp.int32)
    one_hot = (buckets[:, :, None] == jnp.arange(NB, dtype=jnp.int32)).astype(jnp.float32)
    return jnp.einsum("skb,bc->skc", one_hot, dist_table, precision=lax.Precision.HIGHEST)


def head_columns(w_proj, heads):
    by_head = w_proj.reshape(w_proj.shape[0], heads, 2 * HD + VD)
    queries = by_head[:, :, :HD].reshape(-1, heads * HD)
    keys = by_head[:, :, HD : 2 * HD].reshape(-1, heads * HD)
    values = jnp.pad(by_head[:, :, 2 * HD :], ((0, 0), (0, 0), (0, VP - VD)))
    return jnp.concatenate([keys, values.reshape(-1, heads * VP), queries], axis=1)


def whole(memory=pltpu.VMEM):
    return pl.BlockSpec(memory_space=memory)


def local(sequence, deletions, conv_taps, conv_bias, w_proj, w_out, w_pair, dist_table):
    own, width = sequence.shape
    variants = deletions.shape[0]
    heads = w_out.shape[0] // VD
    n_ctx, n_head, n_var = (lax.axis_size(name) for name in ("ctx", "head", "var"))
    step = own // 2
    tokens = n_ctx * own
    mine, ours, core = (lax.axis_index(name) for name in ("ctx", "head", "var"))
    place = jnp.stack([mine, ours]).astype(jnp.int32)

    half = lax.dynamic_slice_in_dim(sequence, core * step, step, 0)
    gathered = lax.all_gather(half, ("ctx", "head", "var"), axis=0, tiled=False)
    gathered = gathered.reshape(n_ctx, n_head, n_var, step, width)
    taps = lax.all_gather(
        jnp.concatenate([conv_taps, conv_bias[None], jnp.zeros((4, width), jnp.float32)], 0),
        "head",
        axis=0,
        tiled=False,
    )
    weights = head_columns(w_proj, heads)
    columns = weights.shape[1]
    base, delta, pooled = pl.pallas_call(
        functools.partial(project_kernel, heads),
        out_shape=(
            jax.ShapeDtypeStruct((tokens, columns), jnp.bfloat16),
            jax.ShapeDtypeStruct((variants, 3 * WIN, columns), jnp.bfloat16),
            jax.ShapeDtypeStruct((variants, own // POOL, width), jnp.bfloat16),
        ),
        in_specs=[whole(pltpu.SMEM), whole(pltpu.SMEM), whole(pl.ANY), whole(), whole()],
        out_specs=(whole(), whole(), whole()),
        scratch_shapes=[
            pltpu.VMEM((n_head, tokens + 2 * step, width), jnp.bfloat16),
            pltpu.VMEM((3 * WIN, n_head * width), jnp.bfloat16),
            pltpu.VMEM((3 * WIN, n_head * width), jnp.bfloat16),
            pltpu.SemaphoreType.DMA((n_ctx * n_var, n_head)),
        ],
        compiler_params=pltpu.CompilerParams(vmem_limit_bytes=56 * MIB),
        name="project",
    )(deletions, place, gathered, taps, weights)

    w_pair_all = lax.all_gather(w_pair, "head", axis=0, tiled=True)
    w_mix = jnp.dot(w_out, w_pair_all, preferred_element_type=jnp.float32).astype(jnp.bfloat16)
    w_mix = jnp.pad(w_mix.reshape(heads, VD, 2 * C), ((0, 0), (0, VP - VD), (0, 0)))
    partial = pl.pallas_call(
        functools.partial(attend_kernel, heads, step),
        out_shape=jax.ShapeDtypeStruct((variants, own // POOL, 2 * C), jnp.bfloat16),
        in_specs=[whole(pltpu.SMEM), whole(pltpu.SMEM)] + [whole()] * 5,
        out_specs=whole(),
        scratch_shapes=[pltpu.VMEM((tokens, columns), jnp.bfloat16)],
        compiler_params=pltpu.CompilerParams(vmem_limit_bytes=56 * MIB),
        name="attend",
    )(deletions, place, base, delta, pooled, w_mix, w_pair)

    pair_rows = own // POOL
    summed = lax.psum_scatter(
        partial.reshape(variants * pair_rows, 2 * C), "head", scatter_dimension=0, tiled=True
    )
    feats = lax.all_gather(summed, ("ctx", "head"), axis=0, tiled=False)
    feats = feats.reshape(n_ctx, variants, pair_rows, 2 * C).astype(jnp.float32)
    col_count = n_ctx * pair_rows // n_head
    row_feats = lax.dynamic_index_in_dim(feats, mine, 0, keepdims=False)[:, :, :C]
    col_feats = lax.dynamic_slice_in_dim(
        feats[..., C:].transpose(1, 0, 2, 3).reshape(variants, n_ctx * pair_rows, C),
        ours * col_count,
        col_count,
        1,
    )
    table = distance_table(
        dist_table, mine * pair_rows, ours * col_count, pair_rows, col_count
    )
    return pl.pallas_call(
        pair_kernel,
        grid=(pair_rows // ROWS,),
        out_shape=jax.ShapeDtypeStruct((variants, pair_rows, col_count, C), jnp.bfloat16),
        in_specs=[
            whole(pltpu.SMEM),
            pl.BlockSpec((variants, ROWS, C), lambda i: (0, i, 0)),
            pl.BlockSpec((variants, col_count, C), lambda i: (0, 0, 0)),
            pl.BlockSpec((SHIFTS, pair_rows + col_count, C), lambda i: (0, 0, 0)),
        ],
        out_specs=pl.BlockSpec((variants, ROWS, col_count, C), lambda i: (0, i, 0, 0)),
        compiler_params=pltpu.CompilerParams(vmem_limit_bytes=48 * MIB),
        name="pair_map",
    )(place, row_feats, col_feats, table)


def solution(mesh):
    in_specs = (
        P("ctx", "head"),
        P("var", None),
        P(None, "head"),
        P("head"),
        P(None, "head"),
        P("head", None),
        P("head", None),
        P(),
    )
    out_specs = P("var", "ctx", "head", None)
    return jax.shard_map(local, mesh=mesh, in_specs=in_specs, out_specs=out_specs, check_vma=False)
```

time: 597 us -> 245 us (0.41)
  waiting for transfers between devices: 407 us -> 95.3 us
  Pallas kernels: 0 us -> 73.9 us
  matrix products: 72.4 us -> 1.47 us
  other arithmetic: 50.2 us -> 4.27 us
  blocking collectives: 10.4 us -> 37.1 us
  local copies, waits for them, and re-layouts: 35.9 us -> 16.6 us
  starting transfers between devices: 6.75 us -> 0.09 us
    all_gather x3 -> x2, waiting for transfers between devices: 235 us -> 77 us  [the longest x1 55.7 us: local(): feats = lax.all_gather(summed, ('ctx', 'head'), axis=0, tiled=False)]
    unnamed x6 -> x3, waiting for transfers between devices: 111 us -> 0.05 us
    pallas_call x0 -> x3, Pallas kernels: none -> 73.9 us  [the longest x1 41.6 us: local(): pl.pallas_call(functools.partial(project_kernel, heads), out_shape=(jax.S...]
    dot_general x12 -> x2, matrix products: 72.4 us -> 1.47 us  [the longest x1 1 us: distance_table(): jnp.einsum('skb,bc->skc', one_hot, dist_table, precision=lax.Precision.HI...]
    ppermute x2 -> x0, waiting for transfers between devices: 34.2 us -> none  [the longest x1 18.8 us: extended(): lax.ppermute(lax.slice_in_dim(block, 0, width, axis=dim), axis, backward)]
    psum x1 -> x0, waiting for transfers between devices: 27.1 us -> none  [local(): lax.psum(partial_value.astype(jnp.bfloat16), 'head').astype(jnp.float32)]
    all_gather x1 -> x2, blocking collectives: 10.4 us -> 37.1 us  [the longest x1 23.4 us: local(): w_pair_all = lax.all_gather(w_pair, 'head', axis=0, tiled=True)]
    reduce_sum x5 -> x0, other arithmetic: 23.5 us -> none  [the longest x4 19.7 us: attend_block(): row_sum = row_sum * shrink + weights.sum(-1)]
  transfers between devices with their start and end apart: 7 -> 3, of which waited for: 7 -> 3; matrix products, arithmetic and copies ran while one was open for 2% -> 8% of each run, Pallas kernels for 0% -> 0%
where the time goes in v1:
time: 245 us; the launch traced here: 242 us
  waiting for transfers between devices  95.3 us (39%)
  Pallas kernels  73.9 us (30%)
  blocking collectives  37.1 us (15%)
  local copies, waits for them, and re-layouts  16.6 us (7%)
  between operations  13.7 us (6%)
  other arithmetic  4.27 us (2%)
    all_gather x1, waiting for transfers between devices, local(): feats = lax.all_gather(summed, ('ctx', 'head'), axis=0, tiled=False)  55.7 us
    pallas_call x1, Pallas kernels, local(): pl.pallas_call(functools.partial(project_kernel, heads), out_shape=(jax.S...  41.6 us
    pallas_call x1, Pallas kernels, local(): pl.pallas_call(functools.partial(attend_kernel, heads, step), out_shape=j...  24.2 us
    all_gather x1, blocking collectives, local(): w_pair_all = lax.all_gather(w_pair, 'head', axis=0, tiled=True)  23.4 us
    all_gather x1, waiting for transfers between devices, local(): gathered = lax.all_gather(half, ('ctx', 'head', 'var'), axis=0, tiled=False)  21.3 us
    reduce_scatter x1, waiting for transfers between devices, local(): lax.psum_scatter(partial.reshape(variants * pair_rows, 2 * C), 'head', sc...  18.3 us
    all_gather x1, blocking collectives, local(): lax.all_gather(jnp.concatenate([conv_taps, conv_bias[None], jnp.zeros((4,...  13.8 us
    pallas_call x1, Pallas kernels, local(): pl.pallas_call(pair_kernel, grid=(pair_rows // ROWS,), out_shape=jax.Shap...  8.08 us
  transfers between devices with their start and end apart: 3, of which 3 were waited for; matrix products, arithmetic and copies ran while one was open for 8% of the time, Pallas kernels for 0%

profile of v1, /device:TPU:0, one launch (start us, length us, event | category | flops | bytes accessed | tf_op | source)
XLA Modules:
  0.0 242.5 jit_solution(6186619267131219148)
XLA Ops:
  6.5 0.0 copy-start
  6.5 0.0 all-gather.6.cloned.1.call-start
  6.5 1.7 constant_dynamic-slice_fusion.1
  8.3 0.0 all-gather.6.cloned.1.call-update
  8.3 0.0 reduce-scatter.2.cloned.1.call-start
  8.3 4.5 %copy.11 = bf16[1536,896]{0,1:T(8,128)(2,1)} copy(bf16[1536,896]{1,0:T(8,128)(2,1)} %param.12) | data formatting | bytes 5505024 | tf_op args[4]
  12.8 2.4 slice.21
  15.2 1.5 fusion.18
  16.7 0.3 copy.18
  17.0 1.2 copy.20
  18.2 0.0 copy-start.7
  18.2 0.0 copy-start.6
  18.2 1.4 pad.8
  19.6 0.0 copy-start.5
  19.6 1.6 copy.19
  21.2 0.0 copy-done.7
  21.2 0.0 copy-start.2
  21.2 0.7 copy.16.dels
  21.8 0.0 copy-done.6
  21.8 23.4 %all_gather.25 = bf16[1536,256]{1,0:T(8,128)(2,1)S(1)} all-gather(bf16[384,256]{1,0:T(8,128)(2,1)} %w_pair.1), channel_id=1, replica_groups=mesh['ctx'=4,'head'=4,'var'=2] {'head'}, dimensions={0}, use_global_device_ids=true | all-gather | bytes 983040 | tf_op jit(solution)/shard_map/all_gather | solution.py:287
  45.2 0.0 copy-done
  45.2 0.5 convolution_convert_fusion
  45.7 0.7 pad.9.w_mix
  46.4 0.1 pad.15.clone
  46.5 0.0 copy-done.5
  46.5 0.1 maximum_maximum_fusion
  46.6 13.8 %all-gather.1 = f32[32,384]{1,0:T(8,128)} all-gather(f32[8,384]{1,0:T(8,128)S(1)} %maximum_maximum_fusion), channel_id=3, replica_groups=mesh['ctx'=4,'head'=4,'var'=2] {'head'}, dimensions={0}, use_global_device_ids=true | all-gather | bytes 61440 | tf_op jit(solution)/shard_map/all_gather | solution.py:260
  60.3 0.7 pad_add_fusion.place
  61.0 0.0 copy-done.2
  61.0 0.0 copy-done.3
  61.0 2.1 pad_maximum_fusion.weights
  63.1 21.3 %all-gather.6.cloned.1.call-done = bf16[8192,384]{1,0:T(8,128)(2,1)} async-done(((bf16[256,384]{1,0:T(8,128)(2,1)}), bf16[8192,384]{1,0:T(8,128)(2,1)}) %all-gather.6.cloned.1.call-update) | async-done | bytes 6291472 | tf_op jit(solution)/shard_map/all_gather | solution.py:258
  84.4 41.6 %project.1 = (bf16[2048,1024]{1,0:T(8,128)(2,1)}, bf16[4,432,1024]{2,1,0:T(8,128)(2,1)}, bf16[4,128,384]{2,1,0:T(8,128)(2,1)}) custom-call(s32[4,2]{1,0:T(4,128)} %copy.16.dels, s32[2]{0:T(128)} %pad_add_fusion.place, bf16[4,4,2,256,384]{4,3,2,1,0:T(8,128)(2,1)} %bitcast.25, f32[4,8,384]{2,1,0:T(8,128)} %bitcast.31, bf16[1536,1024]{1,0:T(8,128)(2,1)} %pad_maximum_fusion.weights), custom_call_target="tpu_custom_call" | custom-call | tf_op jit(solution)/shard_map/project/pallas_call | solution.py:268
  126.0 0.0 copy-start.4
  126.0 24.2 %attend.1 = bf16[4,128,256]{2,1,0:T(8,128)(2,1)} custom-call(s32[4,2]{1,0:T(4,128)} %copy.16.dels, s32[2]{0:T(128)} %pad_add_fusion.place, bf16[2048,1024]{1,0:T(8,128)(2,1)} %get-tuple-element.8.base, bf16[4,432,1024]{2,1,0:T(8,128)(2,1)} %get-tuple-element.9.delta, bf16[4,128,384]{2,1,0:T(8,128)(2,1)} %get-tuple-element.10.pooled, ...), custom_call_target="tpu_custom_call" | custom-call | tf_op jit(solution)/shard_map/attend/pallas_call | solution.py:290
  150.2 0.0 reduce-scatter.2.cloned.1.call-update
  150.2 0.0 all-gather.8.cloned.1.call-start
  150.3 18.3 %reduce-scatter.2.cloned.1.call-done = bf16[128,256]{1,0:T(8,128)(2,1)} async-done(((bf16[512,256]{1,0:T(8,128)(2,1)}), bf16[128,256]{1,0:T(8,128)(2,1)}) %reduce-scatter.2.cloned.1.call-update) | async-done | bytes 65552 | tf_op jit(solution)/shard_map/reduce_scatter | solution.py:301
  168.5 0.0 all-gather.8.cloned.1.call-update
  168.6 0.0 copy-done.4
  168.6 1.0 fusion.table
  169.6 55.7 %all-gather.8.cloned.1.call-done = bf16[2048,256]{1,0:T(8,128)(2,1)} async-done(((bf16[128,256]{1,0:T(8,128)(2,1)}), bf16[2048,256]{1,0:T(8,128)(2,1)}) %all-gather.8.cloned.1.call-update) | async-done | bytes 1048592 | tf_op jit(solution)/shard_map/all_gather | solution.py:304
  225.3 1.4 convert.1
  226.7 0.0 copy-start.1
  226.8 0.1 slice_bitcast_fusion
  226.8 0.1 copy.17
  227.1 0.4 copy-done.1
  227.4 8.1 %pair_map.1 = bf16[4,128,128,128]{3,2,1,0:T(8,128)(2,1)} custom-call(s32[2]{0:T(128)S(1)} %copy-done.1, f32[4,128,128]{2,1,0:T(8,128)S(1)} %slice.23.row_feats, f32[4,128,128]{2,1,0:T(8,128)S(1)} %constant_dynamic-slice_fusion.col_feats, f32[8,256,128]{2,1,0:T(8,128)S(1)} %fusion.table), custom_call_target="tpu_custom_call" | custom-call | tf_op jit(solution)/shard_map/pair_map/pallas_call | solution.py:317
  (7 shorter events, 0.1 us)
Async XLA Ops:
  6.5 38.7 %copy-start = (bf16[384,1536]{1,0:T(8,128)(2,1)S(1)}, bf16[384,1536]{1,0:T(8,128)(2,1)}, u32[]{:S(2)}) copy-start(bf16[384,1536]{1,0:T(8,128)(2,1)} %param.13) | copy-start | bytes 3538948
  6.5 77.8 %all-gather.6.cloned.1.call-start = ((), (), s32[]{:S(2)}) async-start(), calls=%async_computation.2 | async-start | bytes 6488064 | tf_op jit(solution)/shard_map/all_gather | solution.py:258
  8.3 160.3 %reduce-scatter.2.cloned.1.call-start = ((), (), s32[]{:S(2)}) async-start(), calls=%async_computation.1 | async-start | bytes 327680 | tf_op jit(solution)/shard_map/reduce_scatter | solution.py:301
  18.2 3.0 %copy-start.7 = (s32[4,2]{0,1:T(2,128)S(1)}, s32[4,2]{0,1:T(2,128)}, u32[]{:S(2)}) copy-start(s32[4,2]{0,1:T(2,128)} %param.9) | copy-start | bytes 100
  18.2 3.7 %copy-start.6 = (f32[384]{0:T(512)S(1)}, f32[384]{0:T(512)}, u32[]{:S(2)}) copy-start(f32[384]{0:T(512)} %param.11) | copy-start | bytes 4612
  19.6 26.9 %copy-start.5 = (f32[3,384]{1,0:T(4,128)S(1)}, f32[3,384]{1,0:T(4,128)}, u32[]{:S(2)}) copy-start(f32[3,384]{1,0:T(4,128)} %param.10) | copy-start | bytes 13828
  21.2 39.8 %copy-start.2 = (bf16[1536,512]{1,0:T(8,128)(2,1)S(1)}, bf16[1536,512]{1,0:T(8,128)(2,1)}, u32[]{:S(2)}) copy-start(bf16[1536,512]{1,0:T(8,128)(2,1)} %copy.19) | copy-start | bytes 4718596
  21.8 39.2 %copy-start.3 = (bf16[1536,256]{1,0:T(8,128)(2,1)S(1)}, bf16[1536,256]{1,0:T(8,128)(2,1)}, u32[]{:S(2)}) copy-start(bf16[1536,256]{1,0:T(8,128)(2,1)} %copy.20) | copy-start | bytes 2359300
  126.0 42.6 %copy-start.4 = (f32[16,128]{1,0:T(8,128)S(1)}, f32[16,128]{1,0:T(8,128)}, u32[]{:S(2)}) copy-start(f32[16,128]{1,0:T(8,128)} %param.15) | copy-start | bytes 24580
  150.2 75.1 %all-gather.8.cloned.1.call-start = ((), (), s32[]{:S(2)}) async-start(), calls=%async_computation.3 | async-start | bytes 1114112 | tf_op jit(solution)/shard_map/all_gather | solution.py:304
  226.7 0.7 copy-start.1
Sparse Core Ops, SparseCore 0:
  10.4 73.9 all-gather.5
  150.3 18.1 reduce-scatter.1
  171.7 53.5 all-gather.7
